TPU v7x, 32 devices: a whole 2x2x4 slice. The times are simulated.
32 devices in a mesh: dp: 4 (over y, x), shard: 8 (over z, core).
Axes of the slice: x: 2, y: 2, z: 4, core: 2. Of those that a mesh axis runs over, the one named last changes fastest.
Arguments:
- hot_ids: int32 [4096, 8], P(('dp', 'shard')), may hold values from 0 to 4095
- cold_owner: int32 [8192, 1], P(('dp', 'shard')), may hold values from 0 to 7; in each aligned block of 256 rows (0 to 255, 256 to 511, ...) at most 64 rows name the same one
- cold_offset: int32 [8192], P(('dp', 'shard')), may hold values from 0 to 4095
- hot_table: bfloat16 [4096, 128], replicated, may hold values from -2 to 2
- cold_table: bfloat16 [32768, 128], P('shard'), may hold values from -4 to 4
- w_in: bfloat16 [256, 4096], P(None, 'shard'), may hold values from -0.375 to 0.375
- bias_in: bfloat16 [1, 4096], P(None, 'shard'), may hold values from -0.59765625 to 0.59765625
- w_out: bfloat16 [1, 4096], P(None, 'shard'), may hold values from -0.1875 to 0.1875
- cotangent: float32 [4096], P(('dp', 'shard')), may hold values from -10 to 10
Outputs:
- logits: float32 [4096], P(('dp', 'shard'))
- hot_grad: bfloat16 [4096, 128], P('shard')
- cold_grad: bfloat16 [32768, 128], P('shard')
- w_in_grad: float32 [256, 4096], P(None, 'shard')
Inputs may be any that keep to these rules, and one draw needn't show every extreme that they name: `cold_owner`: within the 256 cold lookups of one device no owner is named more than 64 times, a bound that some block reaches.
All inputs are finite; a program needn't handle non-finite values.
Results may differ from a plain program's by a relative error of at most 0.015.
Values may be sent and summed in bfloat16 or wider, within the bound.
A program may use at most 64 MiB of HBM per device.

v0:
```python
import jax
import jax.numpy as jnp
from jax import lax
from jax.sharding import PartitionSpec as P


def contract_rows(left, right):
    return lax.dot_general(
        left, right, (((0,), (0,)), ((), ())), preferred_element_type=jnp.float32
    )


def shards(
    hot_ids, cold_owner, cold_offset, hot_table, cold_table, w_in, bias_in, w_out, cotangent
):
    shard_count = lax.axis_size("shard")
    my_index = lax.axis_index("shard")
    samples_dev = hot_ids.shape[0]
    hot_width = hot_ids.shape[1]
    table_rows = hot_table.shape[0]
    embed = hot_table.shape[1]
    kept_rows = table_rows // shard_count
    owned_rows = cold_table.shape[0]
    row_numbers = jnp.arange(table_rows, dtype=jnp.int32)
    hot_counts = jnp.zeros((samples_dev, table_rows), jnp.float32)
    for lookup in range(hot_width):
        hot_counts = hot_counts + (hot_ids[:, lookup][:, None] == row_numbers[None, :]).astype(
            jnp.float32
        )
    hot_counts = hot_counts.astype(jnp.bfloat16)
    hot_pooled = jnp.dot(hot_counts, hot_table, preferred_element_type=jnp.float32)
    owner_ids = cold_owner[:, 0]
    lookups = owner_ids.shape[0]
    per_sample = lookups // samples_dev
    capacity = max(2, 2 * lookups // shard_count)
    matches = (owner_ids[:, None] == jnp.arange(shard_count, dtype=jnp.int32)[None, :]).astype(
        jnp.int32
    )
    ordinal = jnp.cumsum(matches, axis=0) - 1
    slot_index = jnp.sum(ordinal * matches, axis=1)
    slot_place = owner_ids * capacity + slot_index
    slot_match = slot_place[:, None] == jnp.arange(shard_count * capacity, dtype=jnp.int32)[None, :]
    requests = jnp.sum(jnp.where(slot_match, cold_offset[:, None], 0), axis=0).reshape(
        shard_count, capacity
    )
    present = jnp.sum(slot_match.astype(jnp.int32), axis=0).reshape(shard_count, capacity)
    slot_table = slot_match.astype(jnp.bfloat16)
    offsets = lax.all_to_all(requests, "shard", split_axis=0, concat_axis=0, tiled=True)
    markers = lax.all_to_all(present, "shard", split_axis=0, concat_axis=0, tiled=True)
    fetched = jnp.take(cold_table, offsets, axis=0)
    fetched = jnp.where(markers[:, :, None] > 0, fetched, jnp.zeros_like(fetched))
    answer = lax.all_to_all(fetched, "shard", split_axis=0, concat_axis=0, tiled=True)
    mine = jnp.dot(slot_table, answer.reshape(-1, embed), preferred_element_type=jnp.float32)
    cold_pooled = jnp.sum(mine.reshape(samples_dev, per_sample, embed), axis=1)
    inputs = jnp.concatenate([hot_pooled, cold_pooled], axis=1).astype(jnp.bfloat16)
    group_inputs = lax.all_gather(inputs, "shard", axis=0, tiled=True)
    preact = (
        jnp.dot(group_inputs, w_in, preferred_element_type=jnp.float32)
        + bias_in[0].astype(jnp.float32)[None, :]
    )
    sigma = jax.nn.sigmoid(preact)
    hidden = (preact * sigma).astype(jnp.bfloat16)
    logit_share = jnp.dot(hidden, w_out[0], preferred_element_type=jnp.float32)
    group_logits = lax.psum(logit_share, "shard")
    logits = lax.dynamic_slice_in_dim(group_logits, my_index * samples_dev, samples_dev, 0)
    group_cotangent = lax.all_gather(cotangent, "shard", axis=0, tiled=True)
    slope = sigma * (1.0 + preact * (1.0 - sigma))
    hidden_grad = (group_cotangent[:, None] * w_out[0].astype(jnp.float32)[None, :] * slope).astype(
        jnp.bfloat16
    )
    weight_group = contract_rows(group_inputs, hidden_grad).astype(jnp.bfloat16)
    input_grad = lax.psum_scatter(
        jnp.dot(hidden_grad, w_in.T, preferred_element_type=jnp.float32).astype(jnp.bfloat16),
        "shard",
        scatter_dimension=0,
        tiled=True,
    )
    hot_part = contract_rows(hot_counts, input_grad[:, :embed])
    hot_everywhere = lax.psum(hot_part, ("dp", "shard"))
    hot_total = lax.dynamic_slice_in_dim(hot_everywhere, my_index * kept_rows, kept_rows, 0)
    per_lookup = jnp.repeat(input_grad[:, embed:], per_sample, axis=0)
    outgoing = (
        contract_rows(slot_table, per_lookup)
        .astype(jnp.bfloat16)
        .reshape(shard_count, capacity, embed)
    )
    incoming = lax.all_to_all(outgoing, "shard", split_axis=0, concat_axis=0, tiled=True)
    offset_table = (
        offsets.reshape(-1)[:, None] == jnp.arange(owned_rows, dtype=jnp.int32)[None, :]
    ).astype(jnp.bfloat16)
    cold_part = contract_rows(offset_table, incoming.reshape(-1, embed))
    cold_total, weight_total = (
        lax.psum(cold_part.astype(jnp.bfloat16), "dp").astype(jnp.float32),
        lax.psum(weight_group, "dp").astype(jnp.float32),
    )
    return (logits, hot_total.astype(jnp.bfloat16), cold_total.astype(jnp.bfloat16), weight_total)


def solution(mesh):
    in_specs = (
        P(("dp", "shard"), None),
        P(("dp", "shard"), None),
        P(("dp", "shard")),
        P(),
        P("shard", None),
        P(None, "shard"),
        P(None, "shard"),
        P(None, "shard"),
        P(("dp", "shard")),
    )
    out_specs = (P(("dp", "shard")), P("shard", None), P("shard", None), P(None, "shard"))
    return jax.shard_map(shards, mesh=mesh, in_specs=in_specs, out_specs=out_specs, check_vma=False)
```

profile of v0, /device:TPU:0, one launch (start us, length us, event | category | flops | bytes accessed | tf_op | source)
XLA Modules:
  0.0 214.7 jit_solution(14971163135114629105)
XLA Ops:
  7.2 0.8 fusion.11
  8.0 0.6 reduce-window.6
  8.5 0.2 slice_reduce_fusion
  8.8 0.8 fusion.10
  9.6 0.5 broadcast.99
  10.1 1.3 fusion.14
  11.4 0.8 convert_reduce_fusion
  12.3 0.7 all_to_all.24
  12.9 6.3 %all-to-all-start.1 = ((s32[8,1,64]{2,1,0:T(1,128)}), s32[8,1,64]{2,1,0:T(1,128)S(1)}, u32[]{:S(2)}, u32[]{:S(2)}) async-start(s32[8,1,64]{2,1,0:T(1,128)} %all_to_all.24), calls=%async_computation.1 | async-start | bytes 8192 | tf_op jit(solution)/shard_map/all_to_all | solution.py:48
  19.3 1.0 slice_bitcast_fusion.7
  20.2 0.7 reduce.2
  20.9 0.7 add.104
  21.6 0.7 all_to_all.22
  22.3 0.1 eq.239
  22.4 0.1 copy.20
  22.5 12.3 %all-gather = f32[8,1,128]{2,1,0:T(1,128)S(1)} all-gather(f32[1,1,128]{2,1,0:T(1,128)} %bitcast.77), channel_id=1, replica_groups=mesh['dp'=4,'shard'=8] {'shard'}, dimensions={0}, use_global_device_ids=true | all-gather | bytes 4608 | tf_op jit(solution)/shard_map/all_gather | solution.py:66
  34.8 3.3 %all-to-all-start = ((s32[8,1,64]{2,1,0:T(1,128)}), s32[8,1,64]{2,1,0:T(1,128)S(1)}, u32[]{:S(2)}, u32[]{:S(2)}) async-start(s32[8,1,64]{2,1,0:T(1,128)} %all_to_all.22), calls=%async_computation | async-start | bytes 8192 | tf_op jit(solution)/shard_map/all_to_all | solution.py:49
  38.2 0.1 reshape.125
  38.3 5.3 %all-to-all-done = s32[8,1,64]{2,1,0:T(1,128)S(1)} async-done(((s32[8,1,64]{2,1,0:T(1,128)}), s32[8,1,64]{2,1,0:T(1,128)S(1)}, u32[]{:S(2)}, u32[]{:S(2)}) %all-to-all-start) | async-done | bytes 2080 | tf_op jit(solution)/shard_map/all_to_all | solution.py:49
  43.6 1.3 gather_fusion
  44.9 0.9 select_select_fusion
  45.8 3.4 %all-to-all-start.2 = ((bf16[8,64,128]{2,1,0:T(8,128)(2,1)}), bf16[8,64,128]{2,1,0:T(8,128)(2,1)S(1)}, u32[]{:S(2)}, u32[]{:S(2)}) async-start(bf16[8,64,128]{2,1,0:T(8,128)(2,1)} %select_select_fusion), calls=%async_computation.2 | async-start | bytes 262144 | tf_op jit(solution)/shard_map/all_to_all | solution.py:52
  49.2 0.0 reduce-scatter.2.cloned.1.call-start
  49.2 3.7 %convolution_convert_fusion.3 = bf16[128,128]{0,1:T(8,128)(2,1)S(1)} fusion(bf16[4096,128]{1,0:T(8,128)(2,1)} %param.12, s32[128]{0:T(128)S(1)} %get-tuple-element.16, s32[128]{0:T(128)S(1)} %get-tuple-element.17, s32[128]{0:T(128)S(1)} %get-tuple-element.11, s32[128]{0:T(128)S(1)} %get-tuple-element.12, s32[128]{0:T(128)S(1)} %get-tuple-element.13, ...), kind=kOutput, calls=%fused_computation.21 | convolution fusion | flops 146817024 | bytes 1085440 | tf_op jit(solution)/shard_map/dot_general | solution.py:31
  53.0 2.9 %all-to-all-done.2 = bf16[8,64,128]{2,1,0:T(8,128)(2,1)S(1)} async-done(((bf16[8,64,128]{2,1,0:T(8,128)(2,1)}), bf16[8,64,128]{2,1,0:T(8,128)(2,1)S(1)}, u32[]{:S(2)}, u32[]{:S(2)}) %all-to-all-start.2) | async-done | bytes 131104 | tf_op jit(solution)/shard_map/all_to_all | solution.py:52
  55.9 0.3 convolution_reduce_fusion
  56.1 0.1 copy.22
  56.3 14.0 %all_gather.6 = bf16[1024,256]{0,1:T(8,128)(2,1)S(1)} all-gather(bf16[128,256]{0,1:T(8,128)(2,1)S(1)} %pad_maximum_fusion), channel_id=1, replica_groups=mesh['dp'=4,'shard'=8] {'shard'}, dimensions={0}, use_global_device_ids=true | all-gather | bytes 589824 | tf_op jit(solution)/shard_map/all_gather | solution.py:56
  70.3 2.3 %multiply_convert_fusion = (bf16[1024,512]{1,0:T(8,128)(2,1)S(1)}, f32[1024,512]{1,0:T(8,128)}) fusion(f32[512]{0:T(512)S(1)} %mul.50, f32[1024]{0:T(1024)S(1)} %bitcast.70, f32[512]{0:T(512)S(1)} %bitcast.75, bf16[1024,256]{0,1:T(8,128)(2,1)S(1)} %all_gather.6, bf16[256,512]{1,0:T(8,128)(2,1)S(1)} %copy-done.1), kind=kOutput, calls=%fused_computation.5 | convolution fusion | flops 274202624 | bytes 3940352 | tf_op jit(solution)/shard_map/dot_general | solution.py:58
  72.6 1.3 convolution_convert_fusion
  73.9 0.7 reduce.10
  74.5 0.1 eq.248
  74.6 28.9 %reduce-scatter.2.cloned.1.call-done = bf16[128,256]{1,0:T(8,128)(2,1)} async-done(((bf16[1024,256]{1,0:T(8,128)(2,1)}), bf16[128,256]{1,0:T(8,128)(2,1)}) %reduce-scatter.2.cloned.1.call-update) | async-done | bytes 65552 | tf_op jit(solution)/shard_map/reduce_scatter | solution.py:72
  103.5 0.8 slice.52
  104.3 1.1 convolution_convert_fusion.2
  105.4 3.4 %all-to-all-start.3 = ((bf16[8,64,128]{2,1,0:T(8,128)(2,1)}), bf16[8,64,128]{2,1,0:T(8,128)(2,1)S(1)}, u32[]{:S(2)}, u32[]{:S(2)}) async-start(bf16[8,64,128]{2,1,0:T(8,128)(2,1)} %bitcast.27), calls=%async_computation.4 | async-start | bytes 262144 | tf_op jit(solution)/shard_map/all_to_all | solution.py:87
  108.8 0.0 all-reduce.4.cloned.1.call-start
  108.8 1.2 convolution_convert_fusion.1
  110.0 5.5 %all-to-all-done.3 = bf16[8,64,128]{2,1,0:T(8,128)(2,1)S(1)} async-done(((bf16[8,64,128]{2,1,0:T(8,128)(2,1)}), bf16[8,64,128]{2,1,0:T(8,128)(2,1)S(1)}, u32[]{:S(2)}, u32[]{:S(2)}) %all-to-all-start.3) | async-done | bytes 131104 | tf_op jit(solution)/shard_map/all_to_all | solution.py:87
  115.5 3.4 %fusion.1 = bf16[4096,128]{1,0:T(8,128)(2,1)} fusion(bf16[512,128]{1,0:T(8,128)(2,1)S(1)} %bitcast.62, s32[512]{0:T(512)S(1)} %eq.248), kind=kOutput, calls=%fused_computation.3 | convolution fusion | flops 539492352 | bytes 1181696 | tf_op jit(solution)/shard_map/dot_general | solution.py:8
  118.9 2.3 %fusion.3 = f32[1,1024]{1,0:T(1,128)S(1)} fusion(f32[1024,512]{1,0:T(8,128)} %get-tuple-element.19, f32[512]{0:T(512)S(1)} %bitcast.76, bf16[1,512]{1,0:T(2,128)(2,1)S(1)} %copy-done.3), kind=kOutput, calls=%fused_computation.22 | convolution fusion | flops 4194304 | bytes 2104320 | tf_op jit(solution)/shard_map/dot_general | solution.py:63
  121.2 14.4 %psum.28 = f32[1024]{0:T(1024)S(1)} all-reduce(f32[1024]{0:T(1024)S(1)} %bitcast.71), channel_id=1, replica_groups=mesh['dp'=4,'shard'=8] {'shard'}, use_global_device_ids=true, to_apply=%region_6.7 | all-reduce | flops 1024 | bytes 8192 | tf_op jit(solution)/shard_map/psum | solution.py:64
  135.6 0.6 dynamic_slice.6
  136.2 2.3 %fusion.6 = f32[4096,128]{1,0:T(8,128)S(1)} fusion(s32[128]{0:T(128)S(1)} %get-tuple-element.16, s32[128]{0:T(128)S(1)} %get-tuple-element.17, s32[128]{0:T(128)S(1)} %get-tuple-element.11, s32[128]{0:T(128)S(1)} %get-tuple-element.12, s32[128]{0:T(128)S(1)} %get-tuple-element.13, s32[128]{0:T(128)S(1)} %get-tuple-element.14, ...), kind=kOutput, calls=%fused_computation.28 | convolution fusion | flops 146800640 | bytes 2134016 | tf_op jit(solution)/shard_map/dot_general | solution.py:8
  138.6 63.7 %all-reduce.5 = bf16[4096,128]{1,0:T(8,128)(2,1)} all-reduce(f32[4096,128]{1,0:T(8,128)S(1)} %fusion.6), channel_id=1, replica_groups=mesh['dp'=4,'shard'=8] {'dp','shard'}, use_global_device_ids=true, to_apply=%region_8.9 | all-reduce | flops 524288 | bytes 3145728 | tf_op jit(solution)/shard_map/psum | solution.py:79
  202.3 1.6 dynamic-slice_convert_fusion
  203.8 1.8 convert_element_type.86
  205.6 2.3 %copy.27 = bf16[4096,128]{1,0:T(8,128)(2,1)} copy(bf16[4096,128]{1,0:T(8,128)(2,1)} %get-tuple-element.22) | data formatting | bytes 2097152
  (21 shorter events, 0.2 us)
Async XLA Ops:
  7.2 36.4 %copy-start = (bf16[4096,128]{1,0:T(8,128)(2,1)S(1)}, bf16[4096,128]{1,0:T(8,128)(2,1)}, u32[]{:S(2)}) copy-start(bf16[4096,128]{1,0:T(8,128)(2,1)} %param.13) | copy-start | bytes 3145732
  12.9 21.9 %all-to-all-start.1 = ((s32[8,1,64]{2,1,0:T(1,128)}), s32[8,1,64]{2,1,0:T(1,128)S(1)}, u32[]{:S(2)}, u32[]{:S(2)}) async-start(s32[8,1,64]{2,1,0:T(1,128)} %all_to_all.24), calls=%async_computation.1 | async-start | bytes 8192 | tf_op jit(solution)/shard_map/all_to_all | solution.py:48
  34.8 8.7 %all-to-all-start = ((s32[8,1,64]{2,1,0:T(1,128)}), s32[8,1,64]{2,1,0:T(1,128)S(1)}, u32[]{:S(2)}, u32[]{:S(2)}) async-start(s32[8,1,64]{2,1,0:T(1,128)} %all_to_all.22), calls=%async_computation | async-start | bytes 8192 | tf_op jit(solution)/shard_map/all_to_all | solution.py:49
  45.8 10.1 %all-to-all-start.2 = ((bf16[8,64,128]{2,1,0:T(8,128)(2,1)}), bf16[8,64,128]{2,1,0:T(8,128)(2,1)S(1)}, u32[]{:S(2)}, u32[]{:S(2)}) async-start(bf16[8,64,128]{2,1,0:T(8,128)(2,1)} %select_select_fusion), calls=%async_computation.2 | async-start | bytes 262144 | tf_op jit(solution)/shard_map/all_to_all | solution.py:52
  49.2 54.3 %reduce-scatter.2.cloned.1.call-start = ((), (), s32[]{:S(2)}) async-start(), calls=%async_computation.5 | async-start | bytes 589824 | tf_op jit(solution)/shard_map/reduce_scatter | solution.py:72
  49.2 21.1 %copy-start.1 = (bf16[256,512]{1,0:T(8,128)(2,1)S(1)}, bf16[256,512]{1,0:T(8,128)(2,1)}, u32[]{:S(2)}) copy-start(bf16[256,512]{1,0:T(8,128)(2,1)} %param.14) | copy-start | bytes 786436
  105.4 10.1 %all-to-all-start.3 = ((bf16[8,64,128]{2,1,0:T(8,128)(2,1)}), bf16[8,64,128]{2,1,0:T(8,128)(2,1)S(1)}, u32[]{:S(2)}, u32[]{:S(2)}) async-start(bf16[8,64,128]{2,1,0:T(8,128)(2,1)} %bitcast.27), calls=%async_computation.4 | async-start | bytes 262144 | tf_op jit(solution)/shard_map/all_to_all | solution.py:87
  108.8 95.1 %all-reduce.4.cloned.1.call-start = ((), (), s32[]{:S(2)}) async-start(), calls=%async_computation.6 | async-start | bytes 2621440 | tf_op jit(solution)/shard_map/psum | solution.py:93
  115.5 3.4 %copy-start.3 = (bf16[1,512]{1,0:T(2,128)(2,1)S(1)}, bf16[1,512]{1,0:T(2,128)(2,1)}, u32[]{:S(2)}) copy-start(bf16[1,512]{1,0:T(2,128)(2,1)} %param.16) | copy-start | bytes 3076
  118.9 17.3 %copy-start.2 = (bf16[128,256]{1,0:T(8,128)(2,1)S(1)}, bf16[128,256]{1,0:T(8,128)(2,1)}, u32[]{:S(2)}) copy-start(bf16[128,256]{1,0:T(8,128)(2,1)} %reduce-scatter.2.cloned.1.call-done) | copy-start | bytes 196612
Sparse Core Ops, SparseCore 0:
  74.0 29.4 reduce-scatter.1
  119.0 61.0 all-reduce.3
where the time goes:
time: 216 us; the launch traced here: 215 us
  blocking collectives  104 us (48%)
  waiting for transfers between devices  42.6 us (20%)
  matrix products  17.9 us (8%)
  starting transfers between devices  16.5 us (8%)
  between operations  14.2 us (7%)
  local copies, waits for them, and re-layouts  10.1 us (5%)
  other arithmetic  9.09 us (4%)
    psum x1, blocking collectives, shards(): hot_everywhere = lax.psum(hot_part, ('dp', 'shard'))  63.7 us
    reduce_scatter x1, waiting for transfers between devices, shards(): lax.psum_scatter(jnp.dot(hidden_grad, w_in.T, preferred_element_type=jnp....  28.9 us
    psum x1, blocking collectives, shards(): group_logits = lax.psum(logit_share, 'shard')  14.4 us
    all_gather x1, blocking collectives, shards(): group_inputs = lax.all_gather(inputs, 'shard', axis=0, tiled=True)  14 us
    all_gather x1, blocking collectives, shards(): group_cotangent = lax.all_gather(cotangent, 'shard', axis=0, tiled=True)  12.3 us
    dot_general x4, matrix products, contract_rows(): lax.dot_general(left, right, (((0,), (0,)), ((), ())), preferred_element_...  8.01 us
    all_to_all x1, starting transfers between devices, shards(): lax.all_to_all(requests, 'shard', split_axis=0, concat_axis=0, tiled=True)  6.33 us
    all_to_all x1, waiting for transfers between devices, shards(): lax.all_to_all(outgoing, 'shard', split_axis=0, concat_axis=0, tiled=True)  5.5 us
  transfers between devices with their start and end apart: 6, of which 4 were waited for; matrix products, arithmetic and copies ran while one was open for 7% of the time, Pallas kernels for 0%

commit v1 on v0

--- a/solution.py
+++ b/solution.py
@@ -2,6 +2,18 @@
 import jax.numpy as jnp
 from jax import lax
 from jax.sharding import PartitionSpec as P
+
+
+def cut_along(x, dim, size):
+    dims = x.shape
+    blocks = x.reshape(*dims[:dim], size, dims[dim] // size, *dims[dim + 1 :])
+    return jnp.moveaxis(blocks, dim, 0)
+
+
+def joined_along(tiles, dim):
+    tiles = jnp.moveaxis(tiles, 0, dim)
+    lengths = tiles.shape
+    return tiles.reshape(*lengths[:dim], lengths[dim] * lengths[dim + 1], *lengths[dim + 2 :])
 
 
 def contract_rows(left, right):
@@ -84,7 +96,16 @@
         .astype(jnp.bfloat16)
         .reshape(shard_count, capacity, embed)
     )
-    incoming = lax.all_to_all(outgoing, "shard", split_axis=0, concat_axis=0, tiled=True)
+    devices, index = (lax.axis_size("shard"), lax.axis_index("shard"))
+    blocks = cut_along(outgoing, 0, devices)
+    outs = [blocks[index]]
+    for step in range(1, devices):
+        sent = blocks[(index + step) % devices]
+        outs.append(
+            lax.ppermute(sent, "shard", [(i, (i + step) % devices) for i in range(devices)])
+        )
+    blocks = jnp.stack(outs)[(index - jnp.arange(devices)) % devices]
+    incoming = joined_along(blocks, 0)
     offset_table = (
         offsets.reshape(-1)[:, None] == jnp.arange(owned_rows, dtype=jnp.int32)[None, :]
     ).astype(jnp.bfloat16)

time: 216 us -> 221 us (1.023)
  waiting for transfers between devices: 42.6 us -> 46.5 us
  starting transfers between devices: 16.5 us -> 19.4 us
    ppermute x0 -> x7, waiting for transfers between devices: none -> 9.59 us  [shards(): lax.ppermute(sent, 'shard', [(i, (i + step) % devices) for i in range(dev...]
    ppermute x0 -> x7, starting transfers between devices: none -> 6.27 us  [shards(): lax.ppermute(sent, 'shard', [(i, (i + step) % devices) for i in range(dev...]
    all_to_all x1 -> x0, waiting for transfers between devices: 5.5 us -> none  [shards(): lax.all_to_all(outgoing, 'shard', split_axis=0, concat_axis=0, tiled=True)]
    all_to_all x1 -> x0, starting transfers between devices: 3.37 us -> none  [shards(): lax.all_to_all(outgoing, 'shard', split_axis=0, concat_axis=0, tiled=True)]
  transfers between devices with their start and end apart: 6 -> 12, of which waited for: 4 -> 5; matrix products, arithmetic and copies ran while one was open for 7% -> 7% of each run, Pallas kernels for 0% -> 0%
where the time goes in v1:
time: 221 us
  blocking collectives  103 us (47%)
  waiting for transfers between devices  46.5 us (21%)
  starting transfers between devices  19.4 us (9%)
  matrix products  17.1 us (8%)
  between operations  14.4 us (7%)
  local copies, waits for them, and re-layouts  10.8 us (5%)
  other arithmetic  9.11 us (4%)
    psum x1, blocking collectives, shards(): hot_everywhere = lax.psum(hot_part, ('dp', 'shard'))  62.8 us
    reduce_scatter x1, waiting for transfers between devices, shards(): lax.psum_scatter(jnp.dot(hidden_grad, w_in.T, preferred_element_type=jnp....  28.7 us
    psum x1, blocking collectives, shards(): group_logits = lax.psum(logit_share, 'shard')  14.1 us
    all_gather x1, blocking collectives, shards(): group_inputs = lax.all_gather(inputs, 'shard', axis=0, tiled=True)  14 us
    all_gather x1, blocking collectives, shards(): group_cotangent = lax.all_gather(cotangent, 'shard', axis=0, tiled=True)  12.3 us
    ppermute x7, waiting for transfers between devices, shards(): lax.ppermute(sent, 'shard', [(i, (i + step) % devices) for i in range(dev...  9.59 us
    dot_general x4, matrix products, contract_rows(): lax.dot_general(left, right, (((0,), (0,)), ((), ())), preferred_element_...  7.32 us
    all_to_all x1, starting transfers between devices, shards(): lax.all_to_all(requests, 'shard', split_axis=0, concat_axis=0, tiled=True)  6.33 us
  transfers between devices with their start and end apart: 12, of which 5 were waited for; matrix products, arithmetic and copies ran while one was open for 7% of the time, Pallas kernels for 0%

profile of v1, /device:TPU:0, one launch (start us, length us, event | category | flops | bytes accessed | tf_op | source)
XLA Modules:
  0.0 220.5 jit_solution(12789885536328002633)
XLA Ops:
  7.2 0.8 fusion.11
  8.0 0.6 reduce-window.6
  8.5 0.2 slice_reduce_fusion
  8.8 0.8 fusion.10
  9.6 0.5 broadcast.175
  10.1 1.3 fusion.16
  11.4 0.8 convert_reduce_fusion
  12.3 0.7 all_to_all.21
  12.9 6.3 %all-to-all-start.1 = ((s32[8,1,64]{2,1,0:T(1,128)}), s32[8,1,64]{2,1,0:T(1,128)S(1)}, u32[]{:S(2)}, u32[]{:S(2)}) async-start(s32[8,1,64]{2,1,0:T(1,128)} %all_to_all.21), calls=%async_computation.1 | async-start | bytes 8192 | tf_op jit(solution)/shard_map/all_to_all | solution.py:60
  19.3 1.0 slice_bitcast_fusion.7
  20.2 0.7 reduce.2
  20.9 0.7 add.218
  21.6 0.7 all_to_all.19
  22.3 0.1 eq.249
  22.5 12.3 %all-gather = f32[8,1,128]{2,1,0:T(1,128)S(1)} all-gather(f32[1,1,128]{2,1,0:T(1,128)} %bitcast.110), channel_id=1, replica_groups=mesh['dp'=4,'shard'=8] {'shard'}, dimensions={0}, use_global_device_ids=true | all-gather | bytes 4608 | tf_op jit(solution)/shard_map/all_gather | solution.py:78
  34.8 3.3 %all-to-all-start = ((s32[8,1,64]{2,1,0:T(1,128)}), s32[8,1,64]{2,1,0:T(1,128)S(1)}, u32[]{:S(2)}, u32[]{:S(2)}) async-start(s32[8,1,64]{2,1,0:T(1,128)} %all_to_all.19), calls=%async_computation | async-start | bytes 8192 | tf_op jit(solution)/shard_map/all_to_all | solution.py:61
  38.2 0.1 reshape.166
  38.3 5.3 %all-to-all-done = s32[8,1,64]{2,1,0:T(1,128)S(1)} async-done(((s32[8,1,64]{2,1,0:T(1,128)}), s32[8,1,64]{2,1,0:T(1,128)S(1)}, u32[]{:S(2)}, u32[]{:S(2)}) %all-to-all-start) | async-done | bytes 2080 | tf_op jit(solution)/shard_map/all_to_all | solution.py:61
  43.6 1.3 gather_fusion
  44.9 0.9 select_select_fusion
  45.8 3.4 %all-to-all-start.2 = ((bf16[8,64,128]{2,1,0:T(8,128)(2,1)}), bf16[8,64,128]{2,1,0:T(8,128)(2,1)S(1)}, u32[]{:S(2)}, u32[]{:S(2)}) async-start(bf16[8,64,128]{2,1,0:T(8,128)(2,1)} %select_select_fusion), calls=%async_computation.2 | async-start | bytes 262144 | tf_op jit(solution)/shard_map/all_to_all | solution.py:64
  49.2 3.7 %convolution_convert_fusion.3 = bf16[128,128]{0,1:T(8,128)(2,1)S(1)} fusion(bf16[4096,128]{1,0:T(8,128)(2,1)} %param.12, s32[128]{0:T(128)S(1)} %get-tuple-element.24, s32[128]{0:T(128)S(1)} %get-tuple-element.25, s32[128]{0:T(128)S(1)} %get-tuple-element.19, s32[128]{0:T(128)S(1)} %get-tuple-element.20, s32[128]{0:T(128)S(1)} %get-tuple-element.21, ...), kind=kOutput, calls=%fused_computation.22 | convolution fusion | flops 146817024 | bytes 1085440 | tf_op jit(solution)/shard_map/dot_general | solution.py:43
  53.0 2.9 %all-to-all-done.2 = bf16[8,64,128]{2,1,0:T(8,128)(2,1)S(1)} async-done(((bf16[8,64,128]{2,1,0:T(8,128)(2,1)}), bf16[8,64,128]{2,1,0:T(8,128)(2,1)S(1)}, u32[]{:S(2)}, u32[]{:S(2)}) %all-to-all-start.2) | async-done | bytes 131104 | tf_op jit(solution)/shard_map/all_to_all | solution.py:64
  55.9 0.3 convolution_reduce_fusion
  56.1 0.1 copy.22
  56.3 14.0 %all_gather.6 = bf16[1024,256]{0,1:T(8,128)(2,1)S(1)} all-gather(bf16[128,256]{0,1:T(8,128)(2,1)S(1)} %pad_maximum_fusion), channel_id=1, replica_groups=mesh['dp'=4,'shard'=8] {'shard'}, dimensions={0}, use_global_device_ids=true | all-gather | bytes 589824 | tf_op jit(solution)/shard_map/all_gather | solution.py:68
  70.3 2.3 %multiply_convert_fusion = (bf16[1024,512]{1,0:T(8,128)(2,1)S(1)}, f32[1024,512]{1,0:T(8,128)}) fusion(f32[512]{0:T(512)S(1)} %mul.50, f32[1024]{0:T(1024)S(1)} %bitcast.103, f32[512]{0:T(512)S(1)} %bitcast.108, bf16[1024,256]{0,1:T(8,128)(2,1)S(1)} %all_gather.6, bf16[256,512]{1,0:T(8,128)(2,1)S(1)} %copy-done.1), kind=kOutput, calls=%fused_computation.6 | convolution fusion | flops 274202624 | bytes 3940352 | tf_op jit(solution)/shard_map/dot_general | solution.py:70
  72.6 1.3 convolution_convert_fusion
  74.0 0.7 reduce.10
  74.7 0.1 eq.258
  74.8 28.7 %reduce-scatter.2.cloned.1.call-done = bf16[128,256]{1,0:T(8,128)(2,1)} async-done(((bf16[1024,256]{1,0:T(8,128)(2,1)}), bf16[128,256]{1,0:T(8,128)(2,1)}) %reduce-scatter.2.cloned.1.call-update) | async-done | bytes 65552 | tf_op jit(solution)/shard_map/reduce_scatter | solution.py:84
  103.5 0.8 slice.54
  104.3 0.4 convolution_convert_fusion.2
  104.8 1.1 convolution_convert_fusion.1
  105.9 3.5 %collective-permute-start.6 = (bf16[1,64,128]{2,1,0:T(8,128)(2,1)S(1)}, bf16[1,64,128]{2,1,0:T(8,128)(2,1)S(1)}, u32[]{:S(2)}, u32[]{:S(2)}) collective-permute-start(bf16[1,64,128]{2,1,0:T(8,128)(2,1)S(1)} %get-tuple-element.10), channel_id=1, source_target_pairs={{0,7},{1,0},{2,1},{3,2},{4,3},{5,4},{6,5},{7,6},{8,15},{9,8},{10,9... | collective-permute-start | bytes 49160 | tf_op jit(solution)/shard_map/ppermute | solution.py:105
  109.5 2.7 %collective-permute-start.3 = (bf16[1,64,128]{2,1,0:T(8,128)(2,1)S(1)}, bf16[1,64,128]{2,1,0:T(8,128)(2,1)S(1)}, u32[]{:S(2)}, u32[]{:S(2)}) collective-permute-start(bf16[1,64,128]{2,1,0:T(8,128)(2,1)S(1)} %get-tuple-element.13), channel_id=1, source_target_pairs={{0,4},{1,5},{2,6},{3,7},{4,0},{5,1},{6,2},{7,3},{8,12},{9,13},{10,... | collective-permute-start | bytes 49160 | tf_op jit(solution)/shard_map/ppermute | solution.py:105
  112.1 5.5 %collective-permute-done.1 = bf16[1,64,128]{2,1,0:T(8,128)(2,1)S(1)} collective-permute-done((bf16[1,64,128]{2,1,0:T(8,128)(2,1)S(1)}, bf16[1,64,128]{2,1,0:T(8,128)(2,1)S(1)}, u32[]{:S(2)}, u32[]{:S(2)}) %collective-permute-start.1) | collective-permute-done | bytes 16416 | tf_op jit(solution)/shard_map/ppermute | solution.py:105
  117.7 4.1 %collective-permute-done.2 = bf16[1,64,128]{2,1,0:T(8,128)(2,1)S(1)} collective-permute-done((bf16[1,64,128]{2,1,0:T(8,128)(2,1)S(1)}, bf16[1,64,128]{2,1,0:T(8,128)(2,1)S(1)}, u32[]{:S(2)}, u32[]{:S(2)}) %collective-permute-start.2) | collective-permute-done | bytes 16416 | tf_op jit(solution)/shard_map/ppermute | solution.py:105
  121.8 0.6 gather_fusion.1
  122.4 3.4 %fusion.1 = bf16[4096,128]{1,0:T(8,128)(2,1)} fusion(bf16[512,128]{1,0:T(8,128)(2,1)S(1)} %bitcast.96, s32[512]{0:T(512)S(1)} %eq.258), kind=kOutput, calls=%fused_computation.4 | convolution fusion | flops 539492352 | bytes 1181696 | tf_op jit(solution)/shard_map/dot_general | solution.py:20
  125.9 2.3 %fusion.3 = f32[1,1024]{1,0:T(1,128)S(1)} fusion(f32[1024,512]{1,0:T(8,128)} %get-tuple-element.27, f32[512]{0:T(512)S(1)} %bitcast.109, bf16[1,512]{1,0:T(2,128)(2,1)S(1)} %copy-done.3), kind=kOutput, calls=%fused_computation.23 | convolution fusion | flops 4194304 | bytes 2104320 | tf_op jit(solution)/shard_map/dot_general | solution.py:75
  128.2 14.1 %psum.28 = f32[1024]{0:T(1024)S(1)} all-reduce(f32[1024]{0:T(1024)S(1)} %bitcast.104), channel_id=1, replica_groups=mesh['dp'=4,'shard'=8] {'shard'}, use_global_device_ids=true, to_apply=%region_6.7 | all-reduce | flops 1024 | bytes 8192 | tf_op jit(solution)/shard_map/psum | solution.py:76
  142.3 0.6 dynamic_slice.30
  142.9 2.3 %fusion.6 = f32[4096,128]{1,0:T(8,128)S(1)} fusion(s32[128]{0:T(128)S(1)} %get-tuple-element.24, s32[128]{0:T(128)S(1)} %get-tuple-element.25, s32[128]{0:T(128)S(1)} %get-tuple-element.19, s32[128]{0:T(128)S(1)} %get-tuple-element.20, s32[128]{0:T(128)S(1)} %get-tuple-element.21, s32[128]{0:T(128)S(1)} %get-tuple-element.22, ...), kind=kOutput, calls=%fused_computation.29 | convolution fusion | flops 146800640 | bytes 2134016 | tf_op jit(solution)/shard_map/dot_general | solution.py:20
  145.2 62.8 %all-reduce.5 = bf16[4096,128]{1,0:T(8,128)(2,1)} all-reduce(f32[4096,128]{1,0:T(8,128)S(1)} %fusion.6), channel_id=1, replica_groups=mesh['dp'=4,'shard'=8] {'dp','shard'}, use_global_device_ids=true, to_apply=%region_8.9 | all-reduce | flops 524288 | bytes 3145728 | tf_op jit(solution)/shard_map/psum | solution.py:91
  208.1 1.6 dynamic-slice_convert_fusion
  209.6 1.8 convert_element_type.86
  211.4 2.3 %copy.34 = bf16[4096,128]{1,0:T(8,128)(2,1)} copy(bf16[4096,128]{1,0:T(8,128)(2,1)} %get-tuple-element.30) | data formatting | bytes 2097152
  (44 shorter events, 0.5 us)
Async XLA Ops:
  7.2 36.4 %copy-start = (bf16[4096,128]{1,0:T(8,128)(2,1)S(1)}, bf16[4096,128]{1,0:T(8,128)(2,1)}, u32[]{:S(2)}) copy-start(bf16[4096,128]{1,0:T(8,128)(2,1)} %param.13) | copy-start | bytes 3145732
  12.9 21.9 %all-to-all-start.1 = ((s32[8,1,64]{2,1,0:T(1,128)}), s32[8,1,64]{2,1,0:T(1,128)S(1)}, u32[]{:S(2)}, u32[]{:S(2)}) async-start(s32[8,1,64]{2,1,0:T(1,128)} %all_to_all.21), calls=%async_computation.1 | async-start | bytes 8192 | tf_op jit(solution)/shard_map/all_to_all | solution.py:60
  34.8 8.7 %all-to-all-start = ((s32[8,1,64]{2,1,0:T(1,128)}), s32[8,1,64]{2,1,0:T(1,128)S(1)}, u32[]{:S(2)}, u32[]{:S(2)}) async-start(s32[8,1,64]{2,1,0:T(1,128)} %all_to_all.19), calls=%async_computation | async-start | bytes 8192 | tf_op jit(solution)/shard_map/all_to_all | solution.py:61
  45.8 10.1 %all-to-all-start.2 = ((bf16[8,64,128]{2,1,0:T(8,128)(2,1)}), bf16[8,64,128]{2,1,0:T(8,128)(2,1)S(1)}, u32[]{:S(2)}, u32[]{:S(2)}) async-start(bf16[8,64,128]{2,1,0:T(8,128)(2,1)} %select_select_fusion), calls=%async_computation.2 | async-start | bytes 262144 | tf_op jit(solution)/shard_map/all_to_all | solution.py:64
  49.2 54.3 %reduce-scatter.2.cloned.1.call-start = ((), (), s32[]{:S(2)}) async-start(), calls=%async_computation.4 | async-start | bytes 589824 | tf_op jit(solution)/shard_map/reduce_scatter | solution.py:84
  49.2 21.1 %copy-start.1 = (bf16[256,512]{1,0:T(8,128)(2,1)S(1)}, bf16[256,512]{1,0:T(8,128)(2,1)}, u32[]{:S(2)}) copy-start(bf16[256,512]{1,0:T(8,128)(2,1)} %param.14) | copy-start | bytes 786436
  73.8 135.8 %all-reduce.4.cloned.1.call-start = ((), (), s32[]{:S(2)}) async-start(), calls=%async_computation.5 | async-start | bytes 2621440 | tf_op jit(solution)/shard_map/psum | solution.py:114
  104.7 7.4 %collective-permute-start = (bf16[1,64,128]{2,1,0:T(8,128)(2,1)S(1)}, bf16[1,64,128]{2,1,0:T(8,128)(2,1)S(1)}, u32[]{:S(2)}, u32[]{:S(2)}) collective-permute-start(bf16[1,64,128]{2,1,0:T(8,128)(2,1)S(1)} %get-tuple-element.16), channel_id=1, source_target_pairs={{0,1},{1,2},{2,3},{3,4},{4,5},{5,6},{6,7},{7,0},{8,9},{9,10},{10,1... | collective-permute-start | bytes 49160 | tf_op jit(solution)/shard_map/ppermute | solution.py:105
  105.9 15.9 %collective-permute-start.6 = (bf16[1,64,128]{2,1,0:T(8,128)(2,1)S(1)}, bf16[1,64,128]{2,1,0:T(8,128)(2,1)S(1)}, u32[]{:S(2)}, u32[]{:S(2)}) collective-permute-start(bf16[1,64,128]{2,1,0:T(8,128)(2,1)S(1)} %get-tuple-element.10), channel_id=1, source_target_pairs={{0,7},{1,0},{2,1},{3,2},{4,3},{5,4},{6,5},{7,6},{8,15},{9,8},{10,9... | collective-permute-start | bytes 49160 | tf_op jit(solution)/shard_map/ppermute | solution.py:105
  109.4 12.3 %collective-permute-start.5 = (bf16[1,64,128]{2,1,0:T(8,128)(2,1)S(1)}, bf16[1,64,128]{2,1,0:T(8,128)(2,1)S(1)}, u32[]{:S(2)}, u32[]{:S(2)}) collective-permute-start(bf16[1,64,128]{2,1,0:T(8,128)(2,1)S(1)} %get-tuple-element.11), channel_id=1, source_target_pairs={{0,6},{1,7},{2,0},{3,1},{4,2},{5,3},{6,4},{7,5},{8,14},{9,15},{10,... | collective-permute-start | bytes 49160 | tf_op jit(solution)/shard_map/ppermute | solution.py:105
  109.5 12.3 %collective-permute-start.4 = (bf16[1,64,128]{2,1,0:T(8,128)(2,1)S(1)}, bf16[1,64,128]{2,1,0:T(8,128)(2,1)S(1)}, u32[]{:S(2)}, u32[]{:S(2)}) collective-permute-start(bf16[1,64,128]{2,1,0:T(8,128)(2,1)S(1)} %get-tuple-element.12), channel_id=1, source_target_pairs={{0,5},{1,6},{2,7},{3,0},{4,1},{5,2},{6,3},{7,4},{8,13},{9,14},{10,... | collective-permute-start | bytes 49160 | tf_op jit(solution)/shard_map/ppermute | solution.py:105
  109.5 12.3 %collective-permute-start.3 = (bf16[1,64,128]{2,1,0:T(8,128)(2,1)S(1)}, bf16[1,64,128]{2,1,0:T(8,128)(2,1)S(1)}, u32[]{:S(2)}, u32[]{:S(2)}) collective-permute-start(bf16[1,64,128]{2,1,0:T(8,128)(2,1)S(1)} %get-tuple-element.13), channel_id=1, source_target_pairs={{0,4},{1,5},{2,6},{3,7},{4,0},{5,1},{6,2},{7,3},{8,12},{9,13},{10,... | collective-permute-start | bytes 49160 | tf_op jit(solution)/shard_map/ppermute | solution.py:105
  112.1 5.5 %collective-permute-start.1 = (bf16[1,64,128]{2,1,0:T(8,128)(2,1)S(1)}, bf16[1,64,128]{2,1,0:T(8,128)(2,1)S(1)}, u32[]{:S(2)}, u32[]{:S(2)}) collective-permute-start(bf16[1,64,128]{2,1,0:T(8,128)(2,1)S(1)} %get-tuple-element.15), channel_id=1, source_target_pairs={{0,2},{1,3},{2,4},{3,5},{4,6},{5,7},{6,0},{7,1},{8,10},{9,11},{10,... | collective-permute-start | bytes 49160 | tf_op jit(solution)/shard_map/ppermute | solution.py:105
  117.7 4.1 %collective-permute-start.2 = (bf16[1,64,128]{2,1,0:T(8,128)(2,1)S(1)}, bf16[1,64,128]{2,1,0:T(8,128)(2,1)S(1)}, u32[]{:S(2)}, u32[]{:S(2)}) collective-permute-start(bf16[1,64,128]{2,1,0:T(8,128)(2,1)S(1)} %get-tuple-element.14), channel_id=1, source_target_pairs={{0,3},{1,4},{2,5},{3,6},{4,7},{5,0},{6,1},{7,2},{8,11},{9,12},{10,... | collective-permute-start | bytes 49160 | tf_op jit(solution)/shard_map/ppermute | solution.py:105
  122.4 3.5 %copy-start.3 = (bf16[1,512]{1,0:T(2,128)(2,1)S(1)}, bf16[1,512]{1,0:T(2,128)(2,1)}, u32[]{:S(2)}) copy-start(bf16[1,512]{1,0:T(2,128)(2,1)} %param.16) | copy-start | bytes 3076
  125.9 17.0 %copy-start.2 = (bf16[128,256]{1,0:T(8,128)(2,1)S(1)}, bf16[128,256]{1,0:T(8,128)(2,1)}, u32[]{:S(2)}) copy-start(bf16[128,256]{1,0:T(8,128)(2,1)} %reduce-scatter.2.cloned.1.call-done) | copy-start | bytes 196612
Sparse Core Ops, SparseCore 0:
  74.0 29.4 reduce-scatter.1
  126.0 58.5 all-reduce.3
